TPU v7x, 256 devices: a whole 4x4x8 slice. The times are simulated.
256 devices in a mesh: row: 32 (over x, z_hi, core), col: 8 (over y, z_lo).
Axes of the slice: x: 4, y: 4, z: 8 (z_hi: 4, z_lo: 2; z = z_hi * 2 + z_lo), core: 2. Of those that a mesh axis runs over, the one named last changes fastest.
Arguments:
- activations: bfloat16 [1024, 18432], P('row', 'col'), may hold values from -6 to 6
- out_grads: bfloat16 [1024, 7168], P('col', 'row'), may hold values from -1 to 1
- query_acts: bfloat16 [64, 18432], P('row', 'col'), may hold values from -6 to 6
- query_grads: bfloat16 [64, 7168], P('col', 'row'), may hold values from -1 to 1
- basis_in: bfloat16 [18432, 18432], P('col', 'row'), may hold values from -0.046875 to 0.046875
- basis_out: bfloat16 [7168, 7168], P('row', 'col'), may hold values from -0.0625 to 0.0625
- damping: float32 [1], replicated, may hold values from 0.1 to 1
Outputs:
- corrected: float32 [7168, 18432], P('col', 'row')
All inputs are finite; a program needn't handle non-finite values.
Results may differ from a plain program's by a relative error of at most 0.0044.
Values may be sent and summed in bfloat16 or wider, within the bound.
No kernel may reach another device: no remote copies, remote signals or barrier semaphores. Data moves between devices by JAX's collectives and lax.ppermute only.
A program may use at most 64 MiB of HBM per device.

v0:
```python
import jax
import jax.numpy as jnp
from jax import lax
from jax.sharding import Mesh
from jax.sharding import PartitionSpec as P

TL = 64
EXAMPLES = 16
ROW = ("row_0", "row_1", "row_2")


def in_order(tiles, dim):
    tiles = jnp.moveaxis(tiles, 0, dim)
    shape = tiles.shape
    return tiles.reshape(*shape[:dim], shape[dim] * shape[dim + 1], *shape[dim + 2 :])


def copy_for_each(value, axis):
    peers = lax.axis_size(axis)
    return lax.all_to_all(
        jnp.broadcast_to(value[None], (peers, *value.shape)), axis, 0, 0, tiled=True
    )


def gathered_copies(value, axis, dim):
    return in_order(copy_for_each(value, axis), dim)


def in_blocks(value, dim, peers):
    shape = value.shape
    tiles = value.reshape(*shape[:dim], peers, shape[dim] // peers, *shape[dim + 1 :])
    return jnp.moveaxis(tiles, dim, 0)


def sent_and_summed(value, axis, dim):
    tiles = in_blocks(value, dim, lax.axis_size(axis))
    arrived = lax.all_to_all(tiles, axis, split_axis=0, concat_axis=0, tiled=True)
    return arrived.sum(axis=0)


def summed_rows(value, axes, dim):
    far, near = axes
    tiles = in_blocks(value, dim, lax.axis_size(far))
    nearer = sent_and_summed(tiles, near, dim + 1)
    arrived = lax.all_to_all(nearer, far, split_axis=0, concat_axis=0, tiled=True)
    return arrived.sum(axis=0)


def shards(activations, out_grads, query_acts, query_grads, basis_in, basis_out, damping):
    train_act = activations.shape[0]
    block_act = train_act + query_acts.shape[0]
    act_local = jnp.concatenate([activations, query_acts], 0)
    partial_in = jnp.dot(
        lax.all_gather(act_local, ROW, axis=0, tiled=True),
        basis_in,
        preferred_element_type=jnp.float32,
    )
    train_grad = out_grads.shape[0]
    block_grad = train_grad + query_grads.shape[0]
    grad_local = jnp.concatenate([out_grads, query_grads], 0)
    partial_out = jnp.dot(
        gathered_copies(grad_local, "col", 0), basis_out, preferred_element_type=jnp.float32
    )
    share_in = sent_and_summed(partial_in, "col", 0).astype(jnp.bfloat16)
    summed_in = gathered_copies(share_in, "col", 0)
    share_out = summed_rows(partial_out, (("row_0", "row_1"), "row_2"), 0).astype(jnp.bfloat16)
    summed_out = lax.all_gather(share_out, ROW, axis=0, tiled=True)
    width_in = summed_in.shape[1]
    width_out = summed_out.shape[1]
    groups_in = summed_in.reshape(lax.axis_size(ROW), block_act, width_in)
    rot_act = groups_in[:, :train_act].reshape(-1, width_in)
    q_act = groups_in[:, train_act:].reshape(-1, width_in)
    groups_out = summed_out.reshape(lax.axis_size("col"), block_grad, width_out)
    rot_grad = groups_out[:, :train_grad].reshape(-1, width_out)
    q_grad = groups_out[:, train_grad:].reshape(-1, width_out)

    def accumulate(index, total):
        act_block = lax.dynamic_slice_in_dim(rot_act, index * TL, TL, 0)
        grad_block = lax.dynamic_slice_in_dim(rot_grad, index * TL, TL, 0)
        outer = lax.dot_general(
            grad_block, act_block, (((0,), (0,)), ((), ())), preferred_element_type=jnp.float32
        )
        return total + outer * outer

    moment = (
        lax.fori_loop(0, EXAMPLES, accumulate, jnp.zeros((width_out, width_in), jnp.float32))
        / EXAMPLES
    )
    query = lax.dot_general(
        q_grad, q_act, (((0,), (0,)), ((), ())), preferred_element_type=jnp.float32
    )
    return query / (moment + damping[0])


def solution(mesh):
    finer = Mesh(
        mesh.devices.reshape(4, 4, 2, mesh.shape["col"]), ("row_0", "row_1", "row_2", "col")
    )
    placed = (
        P(ROW, "col"),
        P("col", ROW),
        P(ROW, "col"),
        P("col", ROW),
        P("col", ROW),
        P(ROW, "col"),
        P(),
    )
    return jax.shard_map(
        shards, mesh=finer, in_specs=placed, out_specs=P("col", ROW), check_vma=False
    )
```

profile of v0, /device:TPU:1, one launch (start us, length us, event | category | flops | bytes accessed | tf_op | source)
XLA Modules:
  0.0 283.4 jit_solution(13699588076466373404)
XLA Ops:
  6.5 1.8 maximum_bitcast_fusion
  8.3 0.8 copy.21
  9.2 0.8 pad_maximum_fusion
  10.0 0.1 copy.22
  10.2 15.6 %all_to_all.25 = bf16[8,136,224]{2,1,0:T(8,128)(2,1)} all-to-all(bf16[8,136,224]{2,1,0:T(8,128)(2,1)S(1)} %broadcast_in_dim.6), channel_id=1, replica_groups=mesh['row_0'=4,'row_1'=4,'row_2'=2,'col'=8] {'col'}, dimensions={0} | all-to-all | bytes 974848 | tf_op jit(solution)/shard_map/all_to_all | solution.py:20
  25.8 1.4 dot_general.18
  27.2 1.8 convolution_bitcast_fusion
  29.0 1.3 copy.23
  30.3 9.7 %all_to_all.26 = f32[2,16,34,896]{3,1,2,0:T(8,128)} all-to-all(f32[2,16,34,896]{3,1,2,0:T(8,128)S(1)} %copy.23), channel_id=1, replica_groups=mesh['row_0'=4,'row_1'=4,'row_2'=2,'col'=8] {'row_2'}, dimensions={0} | all-to-all | bytes 7798784 | tf_op jit(solution)/shard_map/all_to_all | solution.py:37
  40.0 3.8 %reduce_sum.27 = f32[16,34,896]{2,0,1:T(8,128)} reduce(f32[2,16,34,896]{3,1,2,0:T(8,128)} %all_to_all.26, f32[]{:T(128)} %constant.33.clone.1), dimensions={0}, to_apply=%region_0.0 | reduce | flops 487424 | bytes 5849092 | tf_op jit(solution)/shard_map/reduce_sum | solution.py:38
  43.9 3.5 %copy.24 = f32[16,34,896]{2,1,0:T(8,128)} copy(f32[16,34,896]{2,0,1:T(8,128)} %reduce_sum.27) | data formatting | bytes 3899392 | tf_op jit(solution)/shard_map/reduce_sum | solution.py:38
  47.4 9.9 %all-to-all-start.2 = ((f32[16,34,896]{2,1,0:T(8,128)}), f32[16,34,896]{2,1,0:T(8,128)}, u32[]{:S(2)}, u32[]{:S(2)}) async-start(f32[16,34,896]{2,1,0:T(8,128)} %copy.24), calls=%async_computation.2 | async-start | bytes 4587520 | tf_op jit(solution)/shard_map/all_to_all | solution.py:45
  57.3 53.6 %all-gather.7.cloned.1.call-done = bf16[32,34,2304]{2,1,0:T(8,128)(2,1)} async-done(((bf16[1,34,2304]{2,1,0:T(8,128)(2,1)}), bf16[32,34,2304]{2,1,0:T(8,128)(2,1)}) %all-gather.7.cloned.1.call-update) | async-done | bytes 5013520 | tf_op jit(solution)/shard_map/all_gather | solution.py:54
  110.9 7.8 %reshape.34 = bf16[1088,2304]{1,0:T(8,128)(2,1)} reshape(bf16[32,34,2304]{2,1,0:T(8,128)(2,1)} %all-gather.7.cloned.1.call-done) | data formatting | bytes 10027008
  118.7 8.1 %fusion.4 = f32[1088,576]{1,0:T(8,128)} fusion(bf16[1088,2304]{1,0:T(8,128)(2,1)} %reshape.34, bf16[2304,576]{0,1:T(8,128)(2,1)S(1)} %copy-done), kind=kOutput, calls=%fused_computation.11 | convolution fusion | flops 2887778304 | bytes 10174464 | tf_op jit(solution)/shard_map/dot_general | solution.py:53
  126.8 3.0 %all-to-all-done.2 = f32[16,34,896]{2,1,0:T(8,128)} async-done(((f32[16,34,896]{2,1,0:T(8,128)}), f32[16,34,896]{2,1,0:T(8,128)}, u32[]{:S(2)}, u32[]{:S(2)}) %all-to-all-start.2) | async-done | bytes 1949728 | tf_op jit(solution)/shard_map/all_to_all | solution.py:45
  129.7 9.8 %all-to-all-start.3 = ((f32[8,136,576]{2,1,0:T(8,128)}), f32[8,136,576]{2,1,0:T(8,128)}, u32[]{:S(2)}, u32[]{:S(2)}) async-start(f32[8,136,576]{2,1,0:T(8,128)} %bitcast.25), calls=%async_computation.3 | async-start | bytes 5570560 | tf_op jit(solution)/shard_map/all_to_all | solution.py:37
  139.6 2.4 reduce_sum.28
  142.0 33.7 %all-to-all-done.3 = f32[8,136,576]{2,1,0:T(8,128)} async-done(((f32[8,136,576]{2,1,0:T(8,128)}), f32[8,136,576]{2,1,0:T(8,128)}, u32[]{:S(2)}, u32[]{:S(2)}) %all-to-all-start.3) | async-done | bytes 2506784 | tf_op jit(solution)/shard_map/all_to_all | solution.py:37
  175.7 1.9 reduce_sum.29
  177.6 1.2 broadcast_in_dim.7
  178.8 4.3 %all-to-all-start.4 = ((bf16[8,136,576]{2,1,0:T(8,128)(2,1)}), bf16[8,136,576]{2,1,0:T(8,128)(2,1)}, u32[]{:S(2)}, u32[]{:S(2)}) async-start(bf16[8,136,576]{2,1,0:T(8,128)(2,1)} %broadcast_in_dim.7), calls=%async_computation.4 | async-start | bytes 2785280 | tf_op jit(solution)/shard_map/all_to_all | solution.py:20
  183.8 20.2 %all-gather.5.cloned.1.call-done = bf16[32,34,896]{2,1,0:T(8,128)(2,1)} async-done(((bf16[1,34,896]{2,1,0:T(8,128)(2,1)}), bf16[32,34,896]{2,1,0:T(8,128)(2,1)}) %all-gather.5.cloned.1.call-update) | async-done | bytes 1949712 | tf_op jit(solution)/shard_map/all_gather | solution.py:67
  204.0 4.0 %reshape.25 = bf16[8,136,896]{2,1,0:T(8,128)(2,1)} reshape(bf16[32,34,896]{2,1,0:T(8,128)(2,1)} %all-gather.5.cloned.1.call-done) | data formatting | bytes 3899392 | tf_op jit(solution)/shard_map/reshape | solution.py:73
  208.0 2.9 %slice.18 = bf16[8,128,896]{2,1,0:T(8,128)(2,1)} slice(bf16[8,136,896]{2,1,0:T(8,128)(2,1)} %reshape.25), slice={[0:8], [0:128], [0:896]} | slice | bytes 3670016 | tf_op jit(solution)/shard_map/slice | solution.py:74
  210.8 0.2 all-to-all-done.4
  211.0 3.5 %reshape_reshape.4 = bf16[32,34,576]{2,1,0:T(8,128)(2,1)} reshape(bf16[8,136,576]{2,1,0:T(8,128)(2,1)} %all-to-all-done.4) | data formatting | bytes 2506752 | tf_op jit(solution)/shard_map/reshape;reshape | solution.py:70
  214.6 1.0 slice.17
  215.6 2.5 slice.19
  218.1 0.1 reshape.28
  218.2 55.0 %while.14 = (s32[]{:T(128)}, f32[896,576]{0,1:T(8,128)}, bf16[1024,896]{1,0:T(8,128)(2,1)}, bf16[1024,576]{1,0:T(8,128)(2,1)}, s32[]{:T(128)}, /*index=5*/s32[]{:T(128)}, s32[]{:T(128)}, s32[]{:T(128)}) while((s32[]{:T(128)}, f32[896,576]{0,1:T(8,128)}, bf16[1024,896]{1,0:T(8,128)(2,1)}, bf16[1024,576]{1,0:T(8,128)(2,1)}, ...), condition=%wide.region_4.0_spmd.clone, body=%wide.region_3.0_spmd.clone.sunk | while | flops 67608584 | bytes 4327060 | solution.py:86
  218.2 2.7 select_add_fusion.2
  220.9 3.5 %select_add_fusion.2 = f32[896,576]{0,1:T(8,128)} fusion(f32[896,576]{0,1:T(8,128)} %get-tuple-element.142, pred[]{:T(512)S(6)} %compare.3, bf16[1024,896]{1,0:T(8,128)(2,1)} %get-tuple-element.151, s32[]{:T(128)S(6)} %select_n.10, bf16[1024,576]{1,0:T(8,128)(2,1)} %get-tuple-element.152), kind=kOutput, calls=%fused_computation.clone.1 | convolution fusion | flops 67608576 | bytes 4326912 | tf_op jit(solution)/shard_map/while/body/eval_jaxpr/dot_general | solution.py:80
  224.4 3.5 %select_add_fusion.2 = f32[896,576]{0,1:T(8,128)} fusion(f32[896,576]{0,1:T(8,128)} %get-tuple-element.142, pred[]{:T(512)S(6)} %compare.3, bf16[1024,896]{1,0:T(8,128)(2,1)} %get-tuple-element.151, s32[]{:T(128)S(6)} %select_n.10, bf16[1024,576]{1,0:T(8,128)(2,1)} %get-tuple-element.152), kind=kOutput, calls=%fused_computation.clone.1 | convolution fusion | flops 67608576 | bytes 4326912 | tf_op jit(solution)/shard_map/while/body/eval_jaxpr/dot_general | solution.py:80
  227.9 3.5 %select_add_fusion.2 = f32[896,576]{0,1:T(8,128)} fusion(f32[896,576]{0,1:T(8,128)} %get-tuple-element.142, pred[]{:T(512)S(6)} %compare.3, bf16[1024,896]{1,0:T(8,128)(2,1)} %get-tuple-element.151, s32[]{:T(128)S(6)} %select_n.10, bf16[1024,576]{1,0:T(8,128)(2,1)} %get-tuple-element.152), kind=kOutput, calls=%fused_computation.clone.1 | convolution fusion | flops 67608576 | bytes 4326912 | tf_op jit(solution)/shard_map/while/body/eval_jaxpr/dot_general | solution.py:80
  231.4 3.5 %select_add_fusion.2 = f32[896,576]{0,1:T(8,128)} fusion(f32[896,576]{0,1:T(8,128)} %get-tuple-element.142, pred[]{:T(512)S(6)} %compare.3, bf16[1024,896]{1,0:T(8,128)(2,1)} %get-tuple-element.151, s32[]{:T(128)S(6)} %select_n.10, bf16[1024,576]{1,0:T(8,128)(2,1)} %get-tuple-element.152), kind=kOutput, calls=%fused_computation.clone.1 | convolution fusion | flops 67608576 | bytes 4326912 | tf_op jit(solution)/shard_map/while/body/eval_jaxpr/dot_general | solution.py:80
  234.9 3.5 %select_add_fusion.2 = f32[896,576]{0,1:T(8,128)} fusion(f32[896,576]{0,1:T(8,128)} %get-tuple-element.142, pred[]{:T(512)S(6)} %compare.3, bf16[1024,896]{1,0:T(8,128)(2,1)} %get-tuple-element.151, s32[]{:T(128)S(6)} %select_n.10, bf16[1024,576]{1,0:T(8,128)(2,1)} %get-tuple-element.152), kind=kOutput, calls=%fused_computation.clone.1 | convolution fusion | flops 67608576 | bytes 4326912 | tf_op jit(solution)/shard_map/while/body/eval_jaxpr/dot_general | solution.py:80
  238.3 3.5 %select_add_fusion.2 = f32[896,576]{0,1:T(8,128)} fusion(f32[896,576]{0,1:T(8,128)} %get-tuple-element.142, pred[]{:T(512)S(6)} %compare.3, bf16[1024,896]{1,0:T(8,128)(2,1)} %get-tuple-element.151, s32[]{:T(128)S(6)} %select_n.10, bf16[1024,576]{1,0:T(8,128)(2,1)} %get-tuple-element.152), kind=kOutput, calls=%fused_computation.clone.1 | convolution fusion | flops 67608576 | bytes 4326912 | tf_op jit(solution)/shard_map/while/body/eval_jaxpr/dot_general | solution.py:80
  241.8 3.5 %select_add_fusion.2 = f32[896,576]{0,1:T(8,128)} fusion(f32[896,576]{0,1:T(8,128)} %get-tuple-element.142, pred[]{:T(512)S(6)} %compare.3, bf16[1024,896]{1,0:T(8,128)(2,1)} %get-tuple-element.151, s32[]{:T(128)S(6)} %select_n.10, bf16[1024,576]{1,0:T(8,128)(2,1)} %get-tuple-element.152), kind=kOutput, calls=%fused_computation.clone.1 | convolution fusion | flops 67608576 | bytes 4326912 | tf_op jit(solution)/shard_map/while/body/eval_jaxpr/dot_general | solution.py:80
  245.3 3.5 %select_add_fusion.2 = f32[896,576]{0,1:T(8,128)} fusion(f32[896,576]{0,1:T(8,128)} %get-tuple-element.142, pred[]{:T(512)S(6)} %compare.3, bf16[1024,896]{1,0:T(8,128)(2,1)} %get-tuple-element.151, s32[]{:T(128)S(6)} %select_n.10, bf16[1024,576]{1,0:T(8,128)(2,1)} %get-tuple-element.152), kind=kOutput, calls=%fused_computation.clone.1 | convolution fusion | flops 67608576 | bytes 4326912 | tf_op jit(solution)/shard_map/while/body/eval_jaxpr/dot_general | solution.py:80
  248.8 3.5 %select_add_fusion.2 = f32[896,576]{0,1:T(8,128)} fusion(f32[896,576]{0,1:T(8,128)} %get-tuple-element.142, pred[]{:T(512)S(6)} %compare.3, bf16[1024,896]{1,0:T(8,128)(2,1)} %get-tuple-element.151, s32[]{:T(128)S(6)} %select_n.10, bf16[1024,576]{1,0:T(8,128)(2,1)} %get-tuple-element.152), kind=kOutput, calls=%fused_computation.clone.1 | convolution fusion | flops 67608576 | bytes 4326912 | tf_op jit(solution)/shard_map/while/body/eval_jaxpr/dot_general | solution.py:80
  252.3 3.5 %select_add_fusion.2 = f32[896,576]{0,1:T(8,128)} fusion(f32[896,576]{0,1:T(8,128)} %get-tuple-element.142, pred[]{:T(512)S(6)} %compare.3, bf16[1024,896]{1,0:T(8,128)(2,1)} %get-tuple-element.151, s32[]{:T(128)S(6)} %select_n.10, bf16[1024,576]{1,0:T(8,128)(2,1)} %get-tuple-element.152), kind=kOutput, calls=%fused_computation.clone.1 | convolution fusion | flops 67608576 | bytes 4326912 | tf_op jit(solution)/shard_map/while/body/eval_jaxpr/dot_general | solution.py:80
  255.8 3.5 %select_add_fusion.2 = f32[896,576]{0,1:T(8,128)} fusion(f32[896,576]{0,1:T(8,128)} %get-tuple-element.142, pred[]{:T(512)S(6)} %compare.3, bf16[1024,896]{1,0:T(8,128)(2,1)} %get-tuple-element.151, s32[]{:T(128)S(6)} %select_n.10, bf16[1024,576]{1,0:T(8,128)(2,1)} %get-tuple-element.152), kind=kOutput, calls=%fused_computation.clone.1 | convolution fusion | flops 67608576 | bytes 4326912 | tf_op jit(solution)/shard_map/while/body/eval_jaxpr/dot_general | solution.py:80
  259.2 3.5 %select_add_fusion.2 = f32[896,576]{0,1:T(8,128)} fusion(f32[896,576]{0,1:T(8,128)} %get-tuple-element.142, pred[]{:T(512)S(6)} %compare.3, bf16[1024,896]{1,0:T(8,128)(2,1)} %get-tuple-element.151, s32[]{:T(128)S(6)} %select_n.10, bf16[1024,576]{1,0:T(8,128)(2,1)} %get-tuple-element.152), kind=kOutput, calls=%fused_computation.clone.1 | convolution fusion | flops 67608576 | bytes 4326912 | tf_op jit(solution)/shard_map/while/body/eval_jaxpr/dot_general | solution.py:80
  262.7 3.5 %select_add_fusion.2 = f32[896,576]{0,1:T(8,128)} fusion(f32[896,576]{0,1:T(8,128)} %get-tuple-element.142, pred[]{:T(512)S(6)} %compare.3, bf16[1024,896]{1,0:T(8,128)(2,1)} %get-tuple-element.151, s32[]{:T(128)S(6)} %select_n.10, bf16[1024,576]{1,0:T(8,128)(2,1)} %get-tuple-element.152), kind=kOutput, calls=%fused_computation.clone.1 | convolution fusion | flops 67608576 | bytes 4326912 | tf_op jit(solution)/shard_map/while/body/eval_jaxpr/dot_general | solution.py:80
  266.2 3.5 %select_add_fusion.2 = f32[896,576]{0,1:T(8,128)} fusion(f32[896,576]{0,1:T(8,128)} %get-tuple-element.142, pred[]{:T(512)S(6)} %compare.3, bf16[1024,896]{1,0:T(8,128)(2,1)} %get-tuple-element.151, s32[]{:T(128)S(6)} %select_n.10, bf16[1024,576]{1,0:T(8,128)(2,1)} %get-tuple-element.152), kind=kOutput, calls=%fused_computation.clone.1 | convolution fusion | flops 67608576 | bytes 4326912 | tf_op jit(solution)/shard_map/while/body/eval_jaxpr/dot_general | solution.py:80
  269.7 3.5 %select_add_fusion.2 = f32[896,576]{0,1:T(8,128)} fusion(f32[896,576]{0,1:T(8,128)} %get-tuple-element.142, pred[]{:T(512)S(6)} %compare.3, bf16[1024,896]{1,0:T(8,128)(2,1)} %get-tuple-element.151, s32[]{:T(128)S(6)} %select_n.10, bf16[1024,576]{1,0:T(8,128)(2,1)} %get-tuple-element.152), kind=kOutput, calls=%fused_computation.clone.1 | convolution fusion | flops 67608576 | bytes 4326912 | tf_op jit(solution)/shard_map/while/body/eval_jaxpr/dot_general | solution.py:80
  273.2 3.4 %add_divide_fusion = f32[896,576]{0,1:T(8,128)} fusion(f32[896,576]{0,1:T(8,128)} %get-tuple-element.84, bf16[64,576]{1,0:T(8,128)(2,1)S(1)} %reshape.28, f32[]{:T(128)} %bitcast.23, bf16[8,136,896]{2,1,0:T(8,128)(2,1)} %reshape.25), kind=kOutput, calls=%fused_computation.5 | convolution fusion | flops 67608576 | bytes 4317696 | tf_op jit(solution)/shard_map/dot_general | solution.py:89
  (8 shorter events, 0.1 us)
Async XLA Ops:
  6.5 112.2 %copy-start = (bf16[2304,576]{0,1:T(8,128)(2,1)S(1)}, bf16[2304,576]{0,1:T(8,128)(2,1)}, u32[]{:S(2)}) copy-start(bf16[2304,576]{0,1:T(8,128)(2,1)} %param.13) | copy-start | bytes 7962628
  6.5 104.4 %all-gather.7.cloned.1.call-start = ((), (), s32[]{:S(2)}) async-start(), calls=%async_computation.6 | async-start | bytes 6082560 | tf_op jit(solution)/shard_map/all_gather | solution.py:54
  47.4 82.3 %all-to-all-start.2 = ((f32[16,34,896]{2,1,0:T(8,128)}), f32[16,34,896]{2,1,0:T(8,128)}, u32[]{:S(2)}, u32[]{:S(2)}) async-start(f32[16,34,896]{2,1,0:T(8,128)} %copy.24), calls=%async_computation.2 | async-start | bytes 4587520 | tf_op jit(solution)/shard_map/all_to_all | solution.py:45
  129.7 45.9 %all-to-all-start.3 = ((f32[8,136,576]{2,1,0:T(8,128)}), f32[8,136,576]{2,1,0:T(8,128)}, u32[]{:S(2)}, u32[]{:S(2)}) async-start(f32[8,136,576]{2,1,0:T(8,128)} %bitcast.25), calls=%async_computation.3 | async-start | bytes 5570560 | tf_op jit(solution)/shard_map/all_to_all | solution.py:37
  139.5 64.4 %all-gather.5.cloned.1.call-start = ((), (), s32[]{:S(2)}) async-start(), calls=%async_computation.5 | async-start | bytes 2365440 | tf_op jit(solution)/shard_map/all_gather | solution.py:67
  178.8 32.2 %all-to-all-start.4 = ((bf16[8,136,576]{2,1,0:T(8,128)(2,1)}), bf16[8,136,576]{2,1,0:T(8,128)(2,1)}, u32[]{:S(2)}, u32[]{:S(2)}) async-start(bf16[8,136,576]{2,1,0:T(8,128)(2,1)} %broadcast_in_dim.7), calls=%async_computation.4 | async-start | bytes 2785280 | tf_op jit(solution)/shard_map/all_to_all | solution.py:20
Sparse Core Ops, SparseCore 0:
  10.0 100.9 all-gather.6
  142.9 61.0 all-gather.4
where the time goes:
time: 285 us; the launch traced here: 283 us
  waiting for transfers between devices  111 us (39%)
  matrix products  68.3 us (24%)
  local copies, waits for them, and re-layouts  30.1 us (11%)
  blocking collectives  25.4 us (9%)
  starting transfers between devices  24 us (8%)
  between operations  14.1 us (5%)
  other arithmetic  10.8 us (4%)
    dot_general x16, matrix products, accumulate(): lax.dot_general(grad_block, act_block, (((0,), (0,)), ((), ())), preferre...  55 us
    all_gather x1, waiting for transfers between devices, shards(): lax.all_gather(act_local, ROW, axis=0, tiled=True)  53.6 us
    all_to_all x1, waiting for transfers between devices, sent_and_summed(): lax.all_to_all(tiles, axis, split_axis=0, concat_axis=0, tiled=True)  33.7 us
    all_gather x1, waiting for transfers between devices, shards(): summed_out = lax.all_gather(share_out, ROW, axis=0, tiled=True)  20.2 us
    all_to_all x1, blocking collectives, copy_for_each(): lax.all_to_all(jnp.broadcast_to(value[None], (peers, *value.shape)), axis...  15.6 us
    all_to_all x1, starting transfers between devices, summed_rows(): lax.all_to_all(nearer, far, split_axis=0, concat_axis=0, tiled=True)  9.91 us
    all_to_all x1, starting transfers between devices, sent_and_summed(): lax.all_to_all(tiles, axis, split_axis=0, concat_axis=0, tiled=True)  9.8 us
    all_to_all x1, blocking collectives, sent_and_summed(): lax.all_to_all(tiles, axis, split_axis=0, concat_axis=0, tiled=True)  9.74 us
  transfers between devices with their start and end apart: 5, of which 5 were waited for; matrix products, arithmetic and copies ran while one was open for 15% of the time, Pallas kernels for 0%

commit v1 on v0

--- a/solution.py
+++ b/solution.py
@@ -64,7 +64,9 @@
     share_in = sent_and_summed(partial_in, "col", 0).astype(jnp.bfloat16)
     summed_in = gathered_copies(share_in, "col", 0)
     share_out = summed_rows(partial_out, (("row_0", "row_1"), "row_2"), 0).astype(jnp.bfloat16)
-    summed_out = lax.all_gather(share_out, ROW, axis=0, tiled=True)
+    summed_out = jnp.concatenate(
+        lax.all_to_all(jnp.stack(lax.axis_size(ROW) * [share_out], 0), ROW, 0, 0), 0
+    )
     width_in = summed_in.shape[1]
     width_out = summed_out.shape[1]
     groups_in = summed_in.reshape(lax.axis_size(ROW), block_act, width_in)

time: 285 us -> 342 us (1.20)
  waiting for transfers between devices: 111 us -> 154 us
  starting transfers between devices: 24 us -> 36.8 us
    all_to_all x0 -> x1, waiting for transfers between devices: none -> 54.2 us  [shards(): lax.all_to_all(jnp.stack(lax.axis_size(ROW) * [share_out], 0), ROW, 0, 0)]
    all_gather x1 -> x0, waiting for transfers between devices: 20.2 us -> none  [shards(): summed_out = lax.all_gather(share_out, ROW, axis=0, tiled=True)]
    all_to_all x0 -> x1, starting transfers between devices: none -> 12.8 us  [shards(): lax.all_to_all(jnp.stack(lax.axis_size(ROW) * [share_out], 0), ROW, 0, 0)]
    all_to_all x1, waiting for transfers between devices: 0.19 us -> 10.8 us  [copy_for_each(): lax.all_to_all(jnp.broadcast_to(value[None], (peers, *value.shape)), axis...]
    another operation x0 -> x2, local copies, waits for them, and re-layouts: none -> 5.59 us  [the longest x1 4 us: shards(): groups_out = summed_out.reshape(lax.axis_size('col'), block_grad, width_out)]
    reshape x1 -> x0, local copies, waits for them, and re-layouts: 3.99 us -> none  [shards(): groups_out = summed_out.reshape(lax.axis_size('col'), block_grad, width_out)]
  transfers between devices with their start and end apart: 5 -> 5, of which waited for: 5 -> 5; matrix products, arithmetic and copies ran while one was open for 15% -> 12% of each run, Pallas kernels for 0% -> 0%
where the time goes in v1:
time: 342 us; the launch traced here: 340 us
  waiting for transfers between devices  154 us (45%)
  matrix products  68.4 us (20%)
  starting transfers between devices  36.8 us (11%)
  local copies, waits for them, and re-layouts  31.7 us (9%)
  blocking collectives  25.4 us (7%)
  between operations  14.1 us (4%)
  other arithmetic  10.1 us (3%)
    dot_general x16, matrix products, accumulate(): lax.dot_general(grad_block, act_block, (((0,), (0,)), ((), ())), preferre...  55 us
    all_to_all x1, waiting for transfers between devices, shards(): lax.all_to_all(jnp.stack(lax.axis_size(ROW) * [share_out], 0), ROW, 0, 0)  54.2 us
    all_gather x1, waiting for transfers between devices, shards(): lax.all_gather(act_local, ROW, axis=0, tiled=True)  53.6 us
    all_to_all x1, waiting for transfers between devices, sent_and_summed(): lax.all_to_all(tiles, axis, split_axis=0, concat_axis=0, tiled=True)  32.3 us
    all_to_all x1, blocking collectives, copy_for_each(): lax.all_to_all(jnp.broadcast_to(value[None], (peers, *value.shape)), axis...  15.6 us
    all_to_all x1, starting transfers between devices, shards(): lax.all_to_all(jnp.stack(lax.axis_size(ROW) * [share_out], 0), ROW, 0, 0)  12.8 us
    all_to_all x1, waiting for transfers between devices, copy_for_each(): lax.all_to_all(jnp.broadcast_to(value[None], (peers, *value.shape)), axis...  10.8 us
    all_to_all x1, starting transfers between devices, summed_rows(): lax.all_to_all(nearer, far, split_axis=0, concat_axis=0, tiled=True)  9.89 us
  transfers between devices with their start and end apart: 5, of which 5 were waited for; matrix products, arithmetic and copies ran while one was open for 12% of the time, Pallas kernels for 0%

profile of v1, /device:TPU:1, one launch (start us, length us, event | category | flops | bytes accessed | tf_op | source)
XLA Modules:
  0.0 340.4 jit_solution(14963299057510112352)
XLA Ops:
  6.5 1.8 maximum_bitcast_fusion
  8.3 0.8 copy.21
  9.2 0.8 pad_maximum_fusion
  10.2 15.6 %all_to_all.30 = bf16[8,136,224]{2,1,0:T(8,128)(2,1)} all-to-all(bf16[8,136,224]{2,1,0:T(8,128)(2,1)S(1)} %broadcast_in_dim.6), channel_id=1, replica_groups=mesh['row_0'=4,'row_1'=4,'row_2'=2,'col'=8] {'col'}, dimensions={0} | all-to-all | bytes 974848 | tf_op jit(solution)/shard_map/all_to_all | solution.py:20
  25.8 1.4 dot_general.18
  27.2 1.9 convolution_bitcast_fusion
  29.0 1.3 copy.23
  30.3 9.8 %all_to_all.31 = f32[2,16,34,896]{3,1,2,0:T(8,128)} all-to-all(f32[2,16,34,896]{3,1,2,0:T(8,128)S(1)} %copy.23), channel_id=1, replica_groups=mesh['row_0'=4,'row_1'=4,'row_2'=2,'col'=8] {'row_2'}, dimensions={0} | all-to-all | bytes 7798784 | tf_op jit(solution)/shard_map/all_to_all | solution.py:37
  40.0 3.8 %reduce_sum.27 = f32[16,34,896]{2,0,1:T(8,128)} reduce(f32[2,16,34,896]{3,1,2,0:T(8,128)} %all_to_all.31, f32[]{:T(128)} %constant.33.clone.1), dimensions={0}, to_apply=%region_0.0 | reduce | flops 487424 | bytes 5849092 | tf_op jit(solution)/shard_map/reduce_sum | solution.py:38
  43.9 3.5 %copy.24 = f32[16,34,896]{2,1,0:T(8,128)} copy(f32[16,34,896]{2,0,1:T(8,128)} %reduce_sum.27) | data formatting | bytes 3899392 | tf_op jit(solution)/shard_map/reduce_sum | solution.py:38
  47.4 9.9 %all-to-all-start.2 = ((f32[16,34,896]{2,1,0:T(8,128)}), f32[16,34,896]{2,1,0:T(8,128)}, u32[]{:S(2)}, u32[]{:S(2)}) async-start(f32[16,34,896]{2,1,0:T(8,128)} %copy.24), calls=%async_computation.2 | async-start | bytes 4587520 | tf_op jit(solution)/shard_map/all_to_all | solution.py:45
  57.3 53.6 %all-gather.3.cloned.1.call-done = bf16[32,34,2304]{2,1,0:T(8,128)(2,1)} async-done(((bf16[1,34,2304]{2,1,0:T(8,128)(2,1)}), bf16[32,34,2304]{2,1,0:T(8,128)(2,1)}) %all-gather.3.cloned.1.call-update) | async-done | bytes 5013520 | tf_op jit(solution)/shard_map/all_gather | solution.py:54
  110.9 7.7 %reshape.30 = bf16[1088,2304]{1,0:T(8,128)(2,1)} reshape(bf16[32,34,2304]{2,1,0:T(8,128)(2,1)} %all-gather.3.cloned.1.call-done) | data formatting | bytes 10027008
  118.7 8.1 %fusion.4 = f32[1088,576]{1,0:T(8,128)} fusion(bf16[1088,2304]{1,0:T(8,128)(2,1)} %reshape.30, bf16[2304,576]{0,1:T(8,128)(2,1)S(1)} %copy-done), kind=kOutput, calls=%fused_computation.10 | convolution fusion | flops 2887778304 | bytes 10174464 | tf_op jit(solution)/shard_map/dot_general | solution.py:53
  126.8 2.9 all-to-all-done.2
  129.7 9.8 %all-to-all-start.4 = ((f32[8,136,576]{2,1,0:T(8,128)}), f32[8,136,576]{2,1,0:T(8,128)}, u32[]{:S(2)}, u32[]{:S(2)}) async-start(f32[8,136,576]{2,1,0:T(8,128)} %bitcast.22), calls=%async_computation.4 | async-start | bytes 5570560 | tf_op jit(solution)/shard_map/all_to_all | solution.py:37
  139.6 1.8 reduce_sum.28
  141.3 32.3 %all-to-all-done.4 = f32[8,136,576]{2,1,0:T(8,128)} async-done(((f32[8,136,576]{2,1,0:T(8,128)}), f32[8,136,576]{2,1,0:T(8,128)}, u32[]{:S(2)}, u32[]{:S(2)}) %all-to-all-start.4) | async-done | bytes 2506784 | tf_op jit(solution)/shard_map/all_to_all | solution.py:37
  173.6 1.6 stack.2
  175.2 12.8 %all-to-all-start.3 = ((bf16[32,34,896]{2,1,0:T(8,128)(2,1)}), bf16[32,34,896]{2,1,0:T(8,128)(2,1)}, u32[]{:S(2)}, u32[]{:S(2)}) async-start(bf16[32,34,896]{2,1,0:T(8,128)(2,1)} %stack.2), calls=%async_computation.3 | async-start | bytes 4587520 | tf_op jit(solution)/shard_map/all_to_all | solution.py:68
  188.0 1.9 reduce_sum.29
  190.0 54.2 %all-to-all-done.3 = bf16[32,34,896]{2,1,0:T(8,128)(2,1)} async-done(((bf16[32,34,896]{2,1,0:T(8,128)(2,1)}), bf16[32,34,896]{2,1,0:T(8,128)(2,1)}, u32[]{:S(2)}, u32[]{:S(2)}) %all-to-all-start.3) | async-done | bytes 1949728 | tf_op jit(solution)/shard_map/all_to_all | solution.py:68
  244.1 1.2 broadcast_in_dim.7
  245.3 4.3 %all-to-all-start.5 = ((bf16[8,136,576]{2,1,0:T(8,128)(2,1)}), bf16[8,136,576]{2,1,0:T(8,128)(2,1)}, u32[]{:S(2)}, u32[]{:S(2)}) async-start(bf16[8,136,576]{2,1,0:T(8,128)(2,1)} %broadcast_in_dim.7), calls=%async_computation.5 | async-start | bytes 2785280 | tf_op jit(solution)/shard_map/all_to_all | solution.py:20
  250.3 4.0 %reshape_reshape.7 = bf16[8,136,896]{2,1,0:T(8,128)(2,1)} reshape(bf16[32,34,896]{2,1,0:T(8,128)(2,1)} %all-to-all-done.3) | data formatting | bytes 3899392 | tf_op jit(solution)/shard_map/reshape;reshape | solution.py:75
  254.3 2.9 slice.18
  257.2 10.8 %all-to-all-done.5 = bf16[8,136,576]{2,1,0:T(8,128)(2,1)} async-done(((bf16[8,136,576]{2,1,0:T(8,128)(2,1)}), bf16[8,136,576]{2,1,0:T(8,128)(2,1)}, u32[]{:S(2)}, u32[]{:S(2)}) %all-to-all-start.5) | async-done | bytes 1253408 | tf_op jit(solution)/shard_map/all_to_all | solution.py:20
  267.9 3.5 %reshape_reshape.8 = bf16[32,34,576]{2,1,0:T(8,128)(2,1)} reshape(bf16[8,136,576]{2,1,0:T(8,128)(2,1)} %all-to-all-done.5) | data formatting | bytes 2506752 | tf_op jit(solution)/shard_map/reshape;reshape | solution.py:72
  271.5 1.0 slice.17
  272.5 2.5 slice.19
  275.1 55.0 %while.14 = (s32[]{:T(128)}, f32[896,576]{0,1:T(8,128)}, bf16[1024,896]{1,0:T(8,128)(2,1)}, bf16[1024,576]{1,0:T(8,128)(2,1)}, s32[]{:T(128)}, /*index=5*/s32[]{:T(128)}, s32[]{:T(128)}, s32[]{:T(128)}) while((s32[]{:T(128)}, f32[896,576]{0,1:T(8,128)}, bf16[1024,896]{1,0:T(8,128)(2,1)}, bf16[1024,576]{1,0:T(8,128)(2,1)}, ...), condition=%wide.region_4.0_spmd.clone, body=%wide.region_3.0_spmd.clone.sunk | while | flops 67608584 | bytes 4327060 | solution.py:88
  275.1 2.7 select_add_fusion.2
  277.9 3.5 %select_add_fusion.2 = f32[896,576]{0,1:T(8,128)} fusion(f32[896,576]{0,1:T(8,128)} %get-tuple-element.142, pred[]{:T(512)S(6)} %compare.3, bf16[1024,896]{1,0:T(8,128)(2,1)} %get-tuple-element.151, s32[]{:T(128)S(6)} %select_n.10, bf16[1024,576]{1,0:T(8,128)(2,1)} %get-tuple-element.152), kind=kOutput, calls=%fused_computation.clone.1 | convolution fusion | flops 67608576 | bytes 4326912 | tf_op jit(solution)/shard_map/while/body/eval_jaxpr/dot_general | solution.py:82
  281.3 3.5 %select_add_fusion.2 = f32[896,576]{0,1:T(8,128)} fusion(f32[896,576]{0,1:T(8,128)} %get-tuple-element.142, pred[]{:T(512)S(6)} %compare.3, bf16[1024,896]{1,0:T(8,128)(2,1)} %get-tuple-element.151, s32[]{:T(128)S(6)} %select_n.10, bf16[1024,576]{1,0:T(8,128)(2,1)} %get-tuple-element.152), kind=kOutput, calls=%fused_computation.clone.1 | convolution fusion | flops 67608576 | bytes 4326912 | tf_op jit(solution)/shard_map/while/body/eval_jaxpr/dot_general | solution.py:82
  284.8 3.5 %select_add_fusion.2 = f32[896,576]{0,1:T(8,128)} fusion(f32[896,576]{0,1:T(8,128)} %get-tuple-element.142, pred[]{:T(512)S(6)} %compare.3, bf16[1024,896]{1,0:T(8,128)(2,1)} %get-tuple-element.151, s32[]{:T(128)S(6)} %select_n.10, bf16[1024,576]{1,0:T(8,128)(2,1)} %get-tuple-element.152), kind=kOutput, calls=%fused_computation.clone.1 | convolution fusion | flops 67608576 | bytes 4326912 | tf_op jit(solution)/shard_map/while/body/eval_jaxpr/dot_general | solution.py:82
  288.3 3.5 %select_add_fusion.2 = f32[896,576]{0,1:T(8,128)} fusion(f32[896,576]{0,1:T(8,128)} %get-tuple-element.142, pred[]{:T(512)S(6)} %compare.3, bf16[1024,896]{1,0:T(8,128)(2,1)} %get-tuple-element.151, s32[]{:T(128)S(6)} %select_n.10, bf16[1024,576]{1,0:T(8,128)(2,1)} %get-tuple-element.152), kind=kOutput, calls=%fused_computation.clone.1 | convolution fusion | flops 67608576 | bytes 4326912 | tf_op jit(solution)/shard_map/while/body/eval_jaxpr/dot_general | solution.py:82
  291.8 3.5 %select_add_fusion.2 = f32[896,576]{0,1:T(8,128)} fusion(f32[896,576]{0,1:T(8,128)} %get-tuple-element.142, pred[]{:T(512)S(6)} %compare.3, bf16[1024,896]{1,0:T(8,128)(2,1)} %get-tuple-element.151, s32[]{:T(128)S(6)} %select_n.10, bf16[1024,576]{1,0:T(8,128)(2,1)} %get-tuple-element.152), kind=kOutput, calls=%fused_computation.clone.1 | convolution fusion | flops 67608576 | bytes 4326912 | tf_op jit(solution)/shard_map/while/body/eval_jaxpr/dot_general | solution.py:82
  295.3 3.5 %select_add_fusion.2 = f32[896,576]{0,1:T(8,128)} fusion(f32[896,576]{0,1:T(8,128)} %get-tuple-element.142, pred[]{:T(512)S(6)} %compare.3, bf16[1024,896]{1,0:T(8,128)(2,1)} %get-tuple-element.151, s32[]{:T(128)S(6)} %select_n.10, bf16[1024,576]{1,0:T(8,128)(2,1)} %get-tuple-element.152), kind=kOutput, calls=%fused_computation.clone.1 | convolution fusion | flops 67608576 | bytes 4326912 | tf_op jit(solution)/shard_map/while/body/eval_jaxpr/dot_general | solution.py:82
  298.7 3.5 %select_add_fusion.2 = f32[896,576]{0,1:T(8,128)} fusion(f32[896,576]{0,1:T(8,128)} %get-tuple-element.142, pred[]{:T(512)S(6)} %compare.3, bf16[1024,896]{1,0:T(8,128)(2,1)} %get-tuple-element.151, s32[]{:T(128)S(6)} %select_n.10, bf16[1024,576]{1,0:T(8,128)(2,1)} %get-tuple-element.152), kind=kOutput, calls=%fused_computation.clone.1 | convolution fusion | flops 67608576 | bytes 4326912 | tf_op jit(solution)/shard_map/while/body/eval_jaxpr/dot_general | solution.py:82
  302.2 3.5 %select_add_fusion.2 = f32[896,576]{0,1:T(8,128)} fusion(f32[896,576]{0,1:T(8,128)} %get-tuple-element.142, pred[]{:T(512)S(6)} %compare.3, bf16[1024,896]{1,0:T(8,128)(2,1)} %get-tuple-element.151, s32[]{:T(128)S(6)} %select_n.10, bf16[1024,576]{1,0:T(8,128)(2,1)} %get-tuple-element.152), kind=kOutput, calls=%fused_computation.clone.1 | convolution fusion | flops 67608576 | bytes 4326912 | tf_op jit(solution)/shard_map/while/body/eval_jaxpr/dot_general | solution.py:82
  305.7 3.5 %select_add_fusion.2 = f32[896,576]{0,1:T(8,128)} fusion(f32[896,576]{0,1:T(8,128)} %get-tuple-element.142, pred[]{:T(512)S(6)} %compare.3, bf16[1024,896]{1,0:T(8,128)(2,1)} %get-tuple-element.151, s32[]{:T(128)S(6)} %select_n.10, bf16[1024,576]{1,0:T(8,128)(2,1)} %get-tuple-element.152), kind=kOutput, calls=%fused_computation.clone.1 | convolution fusion | flops 67608576 | bytes 4326912 | tf_op jit(solution)/shard_map/while/body/eval_jaxpr/dot_general | solution.py:82
  309.2 3.5 %select_add_fusion.2 = f32[896,576]{0,1:T(8,128)} fusion(f32[896,576]{0,1:T(8,128)} %get-tuple-element.142, pred[]{:T(512)S(6)} %compare.3, bf16[1024,896]{1,0:T(8,128)(2,1)} %get-tuple-element.151, s32[]{:T(128)S(6)} %select_n.10, bf16[1024,576]{1,0:T(8,128)(2,1)} %get-tuple-element.152), kind=kOutput, calls=%fused_computation.clone.1 | convolution fusion | flops 67608576 | bytes 4326912 | tf_op jit(solution)/shard_map/while/body/eval_jaxpr/dot_general | solution.py:82
  312.7 3.5 %select_add_fusion.2 = f32[896,576]{0,1:T(8,128)} fusion(f32[896,576]{0,1:T(8,128)} %get-tuple-element.142, pred[]{:T(512)S(6)} %compare.3, bf16[1024,896]{1,0:T(8,128)(2,1)} %get-tuple-element.151, s32[]{:T(128)S(6)} %select_n.10, bf16[1024,576]{1,0:T(8,128)(2,1)} %get-tuple-element.152), kind=kOutput, calls=%fused_computation.clone.1 | convolution fusion | flops 67608576 | bytes 4326912 | tf_op jit(solution)/shard_map/while/body/eval_jaxpr/dot_general | solution.py:82
  316.1 3.5 %select_add_fusion.2 = f32[896,576]{0,1:T(8,128)} fusion(f32[896,576]{0,1:T(8,128)} %get-tuple-element.142, pred[]{:T(512)S(6)} %compare.3, bf16[1024,896]{1,0:T(8,128)(2,1)} %get-tuple-element.151, s32[]{:T(128)S(6)} %select_n.10, bf16[1024,576]{1,0:T(8,128)(2,1)} %get-tuple-element.152), kind=kOutput, calls=%fused_computation.clone.1 | convolution fusion | flops 67608576 | bytes 4326912 | tf_op jit(solution)/shard_map/while/body/eval_jaxpr/dot_general | solution.py:82
  319.6 3.5 %select_add_fusion.2 = f32[896,576]{0,1:T(8,128)} fusion(f32[896,576]{0,1:T(8,128)} %get-tuple-element.142, pred[]{:T(512)S(6)} %compare.3, bf16[1024,896]{1,0:T(8,128)(2,1)} %get-tuple-element.151, s32[]{:T(128)S(6)} %select_n.10, bf16[1024,576]{1,0:T(8,128)(2,1)} %get-tuple-element.152), kind=kOutput, calls=%fused_computation.clone.1 | convolution fusion | flops 67608576 | bytes 4326912 | tf_op jit(solution)/shard_map/while/body/eval_jaxpr/dot_general | solution.py:82
  323.1 3.5 %select_add_fusion.2 = f32[896,576]{0,1:T(8,128)} fusion(f32[896,576]{0,1:T(8,128)} %get-tuple-element.142, pred[]{:T(512)S(6)} %compare.3, bf16[1024,896]{1,0:T(8,128)(2,1)} %get-tuple-element.151, s32[]{:T(128)S(6)} %select_n.10, bf16[1024,576]{1,0:T(8,128)(2,1)} %get-tuple-element.152), kind=kOutput, calls=%fused_computation.clone.1 | convolution fusion | flops 67608576 | bytes 4326912 | tf_op jit(solution)/shard_map/while/body/eval_jaxpr/dot_general | solution.py:82
  326.6 3.5 %select_add_fusion.2 = f32[896,576]{0,1:T(8,128)} fusion(f32[896,576]{0,1:T(8,128)} %get-tuple-element.142, pred[]{:T(512)S(6)} %compare.3, bf16[1024,896]{1,0:T(8,128)(2,1)} %get-tuple-element.151, s32[]{:T(128)S(6)} %select_n.10, bf16[1024,576]{1,0:T(8,128)(2,1)} %get-tuple-element.152), kind=kOutput, calls=%fused_computation.clone.1 | convolution fusion | flops 67608576 | bytes 4326912 | tf_op jit(solution)/shard_map/while/body/eval_jaxpr/dot_general | solution.py:82
  330.1 3.4 %add_divide_fusion = f32[896,576]{0,1:T(8,128)} fusion(f32[896,576]{0,1:T(8,128)} %get-tuple-element.84, bf16[64,576]{1,0:T(8,128)(2,1)S(1)} %reshape.26, f32[]{:T(128)} %bitcast.20, bf16[8,136,896]{2,1,0:T(8,128)(2,1)} %reshape_reshape.7), kind=kOutput, calls=%fused_computation.5 | convolution fusion | flops 67608576 | bytes 4317696 | tf_op jit(solution)/shard_map/dot_general | solution.py:91
  (8 shorter events, 0.2 us)
Async XLA Ops:
  6.5 112.1 %copy-start = (bf16[2304,576]{0,1:T(8,128)(2,1)S(1)}, bf16[2304,576]{0,1:T(8,128)(2,1)}, u32[]{:S(2)}) copy-start(bf16[2304,576]{0,1:T(8,128)(2,1)} %param.13) | copy-start | bytes 7962628
  6.5 104.4 %all-gather.3.cloned.1.call-start = ((), (), s32[]{:S(2)}) async-start(), calls=%async_computation.6 | async-start | bytes 6082560 | tf_op jit(solution)/shard_map/all_gather | solution.py:54
  47.4 82.3 %all-to-all-start.2 = ((f32[16,34,896]{2,1,0:T(8,128)}), f32[16,34,896]{2,1,0:T(8,128)}, u32[]{:S(2)}, u32[]{:S(2)}) async-start(f32[16,34,896]{2,1,0:T(8,128)} %copy.24), calls=%async_computation.2 | async-start | bytes 4587520 | tf_op jit(solution)/shard_map/all_to_all | solution.py:45
  129.7 43.8 %all-to-all-start.4 = ((f32[8,136,576]{2,1,0:T(8,128)}), f32[8,136,576]{2,1,0:T(8,128)}, u32[]{:S(2)}, u32[]{:S(2)}) async-start(f32[8,136,576]{2,1,0:T(8,128)} %bitcast.22), calls=%async_computation.4 | async-start | bytes 5570560 | tf_op jit(solution)/shard_map/all_to_all | solution.py:37
  175.2 68.9 %all-to-all-start.3 = ((bf16[32,34,896]{2,1,0:T(8,128)(2,1)}), bf16[32,34,896]{2,1,0:T(8,128)(2,1)}, u32[]{:S(2)}, u32[]{:S(2)}) async-start(bf16[32,34,896]{2,1,0:T(8,128)(2,1)} %stack.2), calls=%async_computation.3 | async-start | bytes 4587520 | tf_op jit(solution)/shard_map/all_to_all | solution.py:68
  245.3 22.6 %all-to-all-start.5 = ((bf16[8,136,576]{2,1,0:T(8,128)(2,1)}), bf16[8,136,576]{2,1,0:T(8,128)(2,1)}, u32[]{:S(2)}, u32[]{:S(2)}) async-start(bf16[8,136,576]{2,1,0:T(8,128)(2,1)} %broadcast_in_dim.7), calls=%async_computation.5 | async-start | bytes 2785280 | tf_op jit(solution)/shard_map/all_to_all | solution.py:20
Sparse Core Ops, SparseCore 0:
  10.0 100.9 all-gather.2
